TPU v7x, 128 devices: a whole 4x4x4 slice. The times are simulated.
128 devices in a mesh: line: 8 (over y, core), block: 16 (over z, x).
Axes of the slice: x: 4, y: 4, z: 4, core: 2. Of those that a mesh axis runs over, the one named last changes fastest.
Arguments:
- residual: float32 [6, 64, 15, 2048], P(None, 'line', None, 'block'), may hold values from -6 to 6
- adjoint: float32 [6, 64, 15, 2048], P(None, 'line', None, 'block'), may hold values from -6 to 6
- i_factors: float32 [16, 2, 6, 64, 8], P('block', None, None, 'line'), as said below
- k_factors: float32 [8, 2, 6, 2048, 128], P('line', None, None, 'block'), as said below
- couplings: float32 [8, 16, 4, 3, 6], P('line', 'block')
- receptor_cell: int32 [8, 16, 16, 2048], P('line', 'block'), may hold values from 0 to 15359
- send_count: int32 [8, 16, 16], P('line', 'block'), may hold values from 512 to 2048, as said below
- donor_cell: int32 [8, 16, 16, 2048], P('line', 'block'), may hold values from 0 to 13310, as said below
- donor_weight: float32 [8, 16, 3, 16, 2048], P('line', 'block'), may hold values from 0 to 1
Outputs:
- update: float32 [6, 64, 15, 2048], P(None, 'line', None, 'block')
Inputs may be any that keep to these rules, and one draw needn't show every extreme that they name: The first send_count slots of each device for each donor owner are live. In each group along block one donor owner receives exactly 2048 live slots from every source device of the group; every other owner receives at most 1280 live slots from each source, and some source sends exactly that many to some owner. `donor_cell`: numbered within the owner's block; its base cell has i < 7, j < 14 and k < 127 in the block, so that all eight donor cells lie in the block. `receptor_cell`: numbered within the sending device's block; entries of slots that are not live are arbitrary. `i_factors`: each segment matrix is lower triangular with a diagonal between 0.8 and 1.2. `k_factors`: each segment matrix is lower triangular with a diagonal between 0.8 and 1.2.
All inputs are finite; a program needn't handle non-finite values.
Results may differ from a plain program's by a relative error of at most 0.00022.
Values sent between devices are 32-bit elements; how exact they have to be, the bound alone decides.
A program may use at most 320 MiB of HBM per device.

v0:
```python
import jax
import jax.numpy as jnp
from jax import lax
from jax.sharding import PartitionSpec as P


def carried_in(array, axis, combine, identity, reverse):
    peers, index = (lax.axis_size(axis), lax.axis_index(axis))
    everything = jax.tree.map(lambda part: lax.all_gather(part, axis), array)
    start = jax.tree.map(
        lambda part, zero: jnp.broadcast_to(jnp.asarray(zero, part.dtype), part.shape),
        array,
        identity,
    )

    def step(k, before):
        at = peers - 1 - k if reverse else k
        reached = at > index if reverse else at < index
        new = combine(before, jax.tree.map(lambda part: part[at], everything))
        return jax.tree.map(lambda a, b: jnp.where(reached, a, b), new, before)

    return lax.fori_loop(0, peers, step, start)


def coupling_matrix(triple):
    zeros_part = jnp.zeros_like(triple[0])
    upper_row = jnp.stack([triple[0], triple[1]], axis=-1)
    lower_row = jnp.stack([triple[2], zeros_part], axis=-1)
    return jnp.stack([upper_row, lower_row], axis=-2)


def compose(earlier, later):
    first_map, first_vec = earlier
    next_map, next_vec = later
    joined_map = jnp.einsum("fab,fbc->fac", next_map, first_map, precision=lax.Precision.HIGHEST)
    joined_vec = (
        jnp.einsum("fab,fbl->fal", next_map, first_vec, precision=lax.Precision.HIGHEST) + next_vec
    )
    return (joined_map, joined_vec)


def unit_pair(transfer, end_state):
    return (
        jnp.broadcast_to(jnp.eye(2, dtype=jnp.float32), transfer.shape),
        jnp.zeros_like(end_state),
    )


def line_state(transfer, end_state, upward):
    identity = unit_pair(transfer, end_state)
    if upward:
        return carried_in((transfer, end_state), "line", compose, identity, True)[1]
    return carried_in((transfer, end_state), "line", compose, identity, False)[1]


def block_state(transfer, end_state, upward):
    identity = unit_pair(transfer, end_state)
    if upward:
        return carried_in((transfer, end_state), "block", compose, identity, True)[1]
    return carried_in((transfer, end_state), "block", compose, identity, False)[1]


def segment_solve(columns, factor, coupling, last_axis):
    if last_axis:
        homogeneous = jnp.einsum("fpq,flq->flp", factor, columns, precision=lax.Precision.HIGHEST)
        end_state = jnp.stack([homogeneous[:, :, -1], homogeneous[:, :, -2]], axis=1)
    else:
        homogeneous = jnp.einsum("fpq,fql->fpl", factor, columns, precision=lax.Precision.HIGHEST)
        end_state = jnp.stack([homogeneous[:, -1], homogeneous[:, -2]], axis=1)
    influence = jnp.einsum(
        "fpa,fab->fpb", factor[:, :, 0:2], coupling, precision=lax.Precision.HIGHEST
    )
    transfer = -jnp.stack([influence[:, -1], influence[:, -2]], axis=1)
    return (homogeneous, influence, end_state, transfer)


def sweep_i(grid_field, i_factors, couplings):
    fields, cells_i = (grid_field.shape[0], grid_field.shape[1])
    columns = grid_field.reshape(fields, cells_i, -1)
    for upward in (False, True):
        direction = 1 if upward else 0
        oriented = jnp.flip(columns, 1) if upward else columns
        homogeneous, influence, end_state, transfer = segment_solve(
            oriented, i_factors[0, direction], coupling_matrix(couplings[0, 0, direction]), False
        )
        incoming = line_state(transfer, end_state, upward)
        solved = homogeneous - jnp.einsum(
            "fpa,fal->fpl", influence, incoming, precision=lax.Precision.HIGHEST
        )
        columns = jnp.flip(solved, 1) if upward else solved
    return columns.reshape(grid_field.shape)


def sweep_k(grid_field, k_factors, couplings):
    fields, cells_k = (grid_field.shape[0], grid_field.shape[3])
    columns = grid_field.reshape(fields, -1, cells_k)
    for upward in (False, True):
        direction = 3 if upward else 2
        oriented = jnp.flip(columns, 2) if upward else columns
        homogeneous, influence, end_state, transfer = segment_solve(
            oriented, k_factors[0, direction - 2], coupling_matrix(couplings[0, 0, direction]), True
        )
        incoming = block_state(transfer, end_state, upward)
        solved = homogeneous - jnp.einsum(
            "fpa,fal->flp", influence, incoming, precision=lax.Precision.HIGHEST
        )
        columns = jnp.flip(solved, 2) if upward else solved
    return columns.reshape(grid_field.shape)


def spread_donors(right_side, incoming, donor_cell, donor_weight, cells_j, cells_k):
    fields = right_side.shape[0]
    base_cell = donor_cell.reshape(-1)
    fractions = donor_weight.reshape(3, -1)
    values = incoming.reshape(fields, -1)
    index_list = []
    weight_list = []
    for corner in range(8):
        step_i = corner // 4
        step_j = corner // 2 % 2
        step_k = corner % 2
        along_i = fractions[0] if step_i else 1.0 - fractions[0]
        along_j = fractions[1] if step_j else 1.0 - fractions[1]
        along_k = fractions[2] if step_k else 1.0 - fractions[2]
        weight_list.append(along_i * along_j * along_k)
        index_list.append(base_cell + step_i * cells_j * cells_k + step_j * cells_k + step_k)
    targets = jnp.concatenate(index_list)
    weights = jnp.concatenate(weight_list)
    spread = jnp.tile(values, (1, 8)) * weights[None, :]
    return right_side.at[:, targets].add(spread)


def per_device(
    residual,
    adjoint,
    i_factors,
    k_factors,
    couplings,
    receptor_cell,
    send_count,
    donor_cell,
    donor_weight,
):
    fields, cells_i, cells_j, cells_k = adjoint.shape
    owners, capacity = (receptor_cell.shape[2], receptor_cell.shape[3])
    flat_adjoint = adjoint.reshape(fields, -1)
    receptor_index = receptor_cell.reshape(-1)
    outgoing = jnp.take(flat_adjoint, receptor_index, axis=1).reshape(fields, owners, capacity)
    counts = send_count.reshape(owners)
    active_slot = jnp.arange(capacity, dtype=jnp.int32)[None, :] < counts[:, None]
    outgoing = jnp.where(active_slot[None], outgoing, 0.0)
    incoming = lax.all_to_all(outgoing, "block", split_axis=1, concat_axis=1, tiled=True)
    combined = spread_donors(
        residual.reshape(fields, -1),
        incoming,
        donor_cell[0, 0],
        donor_weight[0, 0],
        cells_j,
        cells_k,
    )
    right_side = combined.reshape(residual.shape)
    after_i = sweep_i(right_side, i_factors, couplings)
    return sweep_k(after_i, k_factors, couplings)


def solution(mesh):
    return jax.shard_map(
        per_device,
        mesh=mesh,
        in_specs=(
            P(None, "line", None, "block"),
            P(None, "line", None, "block"),
            P("block", None, None, "line", None),
            P("line", None, None, "block", None),
            P("line", "block", None, None, None),
            P("line", "block", None, None),
            P("line", "block", None),
            P("line", "block", None, None),
            P("line", "block", None, None, None),
        ),
        out_specs=P(None, "line", None, "block"),
        check_vma=False,
    )
```

profile of v0, /device:TPU:0, one launch (start us, length us, event | category | flops | bytes accessed | tf_op | source)
XLA Modules:
  0.0 1832.1 jit_solution(17576297799281508507)
XLA Ops:
  0.0 1.0 copy.165
  1.0 1.0 iota_compare_fusion
  2.1 5.4 copy.132
  7.7 111.6 %gather_fusion = f32[32768,6]{1,0:T(8,128)} fusion(f32[6,15360]{0,1:T(8,128)} %bitcast.203, s32[32768]{0:T(1024)S(1)} %broadcast_clamp_fusion), kind=kCustom, calls=%fused_computation | custom fusion | bytes 1703936 | tf_op jit(solution)/shard_map/jit(_take)/gather | solution.py:148
  119.3 10.0 copy.133
  129.3 1.2 select_select_fusion
  130.5 8.0 all-to-all-start
  138.8 1.1 slice_bitcast_fusion.4
  145.9 2.0 compare_select_fusion
  147.8 5.4 copy.131
  153.9 12.1 all_gather.40
  166.6 11.2 all_gather.43
  179.0 23.7 %all_gather.46 = f32[16,6,2,2]{1,3,2,0:T(2,128)S(1)} all-gather(f32[1,6,2,2]{1,3,2,0:T(2,128)S(1)} %maximum_negate_fusion.2), channel_id=1, replica_groups=mesh['line'=8,'block'=16] {'block'}, dimensions={0}, use_global_device_ids=true | all-gather | bytes 1632 | tf_op jit(solution)/shard_map/all_gather | solution.py:9
  202.8 0.7 fusion.22
  203.8 22.6 %all_gather.49 = f32[16,6,2,2]{1,3,2,0:T(2,128)S(1)} all-gather(f32[1,6,2,2]{1,3,2,0:T(2,128)S(1)} %maximum_negate_fusion.3), channel_id=1, replica_groups=mesh['line'=8,'block'=16] {'block'}, dimensions={0}, use_global_device_ids=true | all-gather | bytes 1632 | tf_op jit(solution)/shard_map/all_gather | solution.py:9
  227.1 9.0 copy.134
  236.1 88.5 %bitcast_multiply_fusion = f32[6,262144]{0,1:T(8,128)} fusion(f32[262144]{0:T(1024)} %multiply_dynamic-update-slice_fusion, f32[6,32768]{0,1:T(8,128)} %copy.134), kind=kLoop, calls=%fused_computation.32 | loop fusion | flops 1572864 | bytes 8126464 | tf_op jit(solution)/shard_map/mul | solution.py:129
  324.5 1401.8 %scatter_custom_fusion = f32[6,15360]{0,1:T(8,128)} fusion(f32[6,15360]{0,1:T(8,128)} %bitcast.204, s32[262144]{0:T(1024)} %bitcast.232, f32[6,262144]{0,1:T(8,128)} %bitcast_multiply_fusion), kind=kCustom, calls=%fused_computation.30 | custom fusion | flops 1572864 | bytes 134586368 | tf_op jit(solution)/shard_map/scatter-add | solution.py:130
  1726.3 5.0 copy.135
  1732.0 13.5 all-gather
  1745.5 5.0 while.60
  1752.0 13.3 all-gather.1
  1765.3 5.0 while.61
  1771.3 0.8 fusion.30
  1772.6 21.4 %all-gather.2 = f32[96,2,120]{2,1,0:T(2,128)S(1)} all-gather(f32[6,2,120]{2,1,0:T(2,128)S(1)} %pad_maximum_fusion.2), channel_id=4, replica_groups=mesh['line'=8,'block'=16] {'block'}, dimensions={0}, use_global_device_ids=true | all-gather | bytes 97920 | tf_op jit(solution)/shard_map/all_gather | solution.py:9
  1794.0 5.0 while.62
  1799.1 0.8 convolution_subtract_fusion.3
  1800.4 0.8 fusion.31
  1801.8 23.0 %all-gather.3 = f32[96,2,120]{2,1,0:T(2,128)S(1)} all-gather(f32[6,2,120]{2,1,0:T(2,128)S(1)} %pad_maximum_fusion.3), channel_id=5, replica_groups=mesh['line'=8,'block'=16] {'block'}, dimensions={0}, use_global_device_ids=true | all-gather | bytes 97920 | tf_op jit(solution)/shard_map/all_gather | solution.py:9
  1824.7 5.1 while.63
  1829.9 0.8 convolution_subtract_fusion.2
  1831.3 0.9 copy.152
  (291 shorter events, 33.3 us)
Async XLA Ops:
  7.5 131.0 %copy-start.1 = (s32[1,1,16,2048]{3,2,1,0:T(8,128)S(1)}, s32[1,1,16,2048]{3,2,1,0:T(8,128)}, u32[]{:S(2)}) copy-start(s32[1,1,16,2048]{3,2,1,0:T(8,128)} %param.24) | copy-start | bytes 393220
  129.3 24.0 %copy-start.3 = (f32[1,1,4,3,6]{4,2,3,1,0:T(4,128)S(1)}, f32[1,1,4,3,6]{4,2,3,1,0:T(4,128)}, u32[]{:S(2)}) copy-start(f32[1,1,4,3,6]{4,2,3,1,0:T(4,128)} %param.21) | copy-start | bytes 868
  129.3 24.1 %copy-start.2 = (f32[1,2,6,8,8]{4,3,2,1,0:T(8,128)S(1)}, f32[1,2,6,8,8]{4,3,2,1,0:T(8,128)}, u32[]{:S(2)}) copy-start(f32[1,2,6,8,8]{4,3,2,1,0:T(8,128)} %param.19) | copy-start | bytes 9220
  129.3 48.6 %copy-start = (f32[1,2,6,128,128]{4,3,2,1,0:T(8,128)S(1)}, f32[1,2,6,128,128]{4,3,2,1,0:T(8,128)}, u32[]{:S(2)}) copy-start(f32[1,2,6,128,128]{4,3,2,1,0:T(8,128)} %param.20) | copy-start | bytes 2359300
  130.5 96.6 %all-to-all-start = ((f32[6,16,2048]{2,0,1:T(8,128)}), f32[6,16,2048]{2,0,1:T(8,128)S(1)}, u32[]{:S(2)}, u32[]{:S(2)}) async-start(f32[6,16,2048]{2,0,1:T(8,128)} %select_select_fusion), calls=%async_computation | async-start | bytes 2097152 | tf_op jit(solution)/shard_map/all_to_all | solution.py:152
where the time goes:
time: 1830 us
  other arithmetic  1500 us (82%)
  local copies, waits for them, and re-layouts  161 us (9%)
  blocking collectives  141 us (8%)
  matrix products  20.2 us (1%)
    scatter-add x1, other arithmetic, spread_donors(): return right_side.at[:, targets].add(spread)  1400 us
    all_gather x8, blocking collectives, carried_in(): everything = jax.tree.map(lambda part: lax.all_gather(part, axis), array)  141 us
    gather x2, local copies, waits for them, and re-layouts, per_device(): jnp.take(flat_adjoint, receptor_index, axis=1)  122 us
    mul x1, other arithmetic, spread_donors(): spread = jnp.tile(values, (1, 8)) * weights[None, :]  88.5 us
  transfers between devices with their start and end apart: 1, of which 0 were waited for; matrix products, arithmetic and copies ran while one was open for 1% of the time, Pallas kernels for 0%

commit v1 on v0

v1 whole, which is shorter than its diff:
```python
import functools

import jax
import jax.numpy as jnp
from jax import lax
from jax.experimental import pallas as pl
from jax.experimental.pallas import tpu as pltpu
from jax.sharding import PartitionSpec as P

F32, BF = jnp.float32, jnp.bfloat16
FIELDS, CI, CJ, CK, CAP = 6, 8, 15, 128, 2048
LINES, BLOCKS = 8, 16
HIGHEST = lax.Precision.HIGHEST
MESH = pl.DeviceIdType.MESH


def iota(shape, axis):
    return lax.broadcasted_iota(jnp.int32, shape, axis)


def split(x):
    high = x.astype(BF)
    return high, (x - high.astype(F32)).astype(BF)


def as_bf(x):
    return x.astype(F32).astype(BF)


def mm(a, b):
    return jnp.dot(a, b, precision=HIGHEST, preferred_element_type=F32)


def mm_nt(a, b):
    return lax.dot_general(
        a, b, (((1,), (1,)), ((), ())), precision=HIGHEST, preferred_element_type=F32
    )


def mm_tn(a, b):
    return lax.dot_general(
        a, b, (((0,), (0,)), ((), ())), precision=HIGHEST, preferred_element_type=F32
    )


def cell_parts(cell):
    ij = cell >> 7
    i = (ij * 137) >> 11
    return i, ij - i * CJ, cell & 127


def gather_kernel(adj_ref, cell_ref, count_ref, out_ref, table, where_ref):
    for f in range(FIELDS):
        planes = [adj_ref[f, j] for j in range(CJ)] + [jnp.zeros((CI, CK), F32)]
        for half in range(2):
            high, low = split(jnp.concatenate(planes[8 * half : 8 * half + 8], 0))
            row, col = f * 64, half * CK
            table[row : row + 64, col : col + CK] = high
            table[row : row + 64, 256 + col : 256 + col + CK] = low
    i, j, k = cell_parts(cell_ref[...])
    where_ref[0] = (j & 7) * CI + i
    where_ref[1] = (j >> 3) * CK + k

    def owner(s, carry):
        C = CAP
        group = jnp.broadcast_to(where_ref[0, pl.ds(s, 1), :], (64, C))
        slot = as_bf(jnp.broadcast_to(where_ref[1, pl.ds(s, 1), :], (16, C)))
        one, zero = jnp.ones((16, C), BF), jnp.zeros((16, C), BF)
        base = iota((16, C), 0)
        hot = [jnp.where(as_bf(base + 16 * n) == slot, one, zero) for n in range(16)]
        hot = jnp.concatenate(hot, 0)
        found = jnp.dot(
            table[...], jnp.concatenate([hot, hot], 0), preferred_element_type=F32
        ).reshape(FIELDS, 64, C)
        mine = iota((64, C), 0) == group
        live = iota((1, C), 1) < count_ref[s]
        for f in range(FIELDS):
            picked = jnp.sum(jnp.where(mine, found[f], 0.0), axis=0, keepdims=True)
            out_ref[s, f : f + 1, :] = jnp.where(live, picked, 0.0)
        return carry

    lax.fori_loop(0, BLOCKS, owner, 0)


def gather(adjoint, receptor_cell, send_count):
    vmem = pl.BlockSpec(memory_space=pltpu.VMEM)
    return pl.pallas_call(
        gather_kernel,
        out_shape=jax.ShapeDtypeStruct((BLOCKS, FIELDS, CAP), F32),
        in_specs=[vmem, vmem, pl.BlockSpec(memory_space=pltpu.SMEM)],
        out_specs=vmem,
        scratch_shapes=[
            pltpu.VMEM((FIELDS * 64, 512), BF),
            pltpu.VMEM((2, BLOCKS, CAP), jnp.int32),
        ],
        compiler_params=pltpu.CompilerParams(vmem_limit_bytes=56 * 2**20),
        name="gather",
    )(adjoint, receptor_cell, send_count)


def scatter_all(inc_ref, cell_ref, weight_ref, acc, place):
    i, j, k = cell_parts(cell_ref[...])
    upper = jnp.where(j >= 7, 1, 0)
    place[0] = i
    place[1] = j - 7 * upper
    place[2] = upper * CK + k
    acc[...] = jnp.zeros_like(acc)

    def source(s, carry):
        C = CAP

        def row(ref, a, n):
            return jnp.broadcast_to(ref[a, pl.ds(s, 1), :], (n, C))

        at = iota((8, C), 0)

        def hat(base, t):
            return jnp.where(at == base, 1.0 - t, jnp.where(at == base + 1, t, 0.0))

        wi = hat(row(place, 0, 8), row(weight_ref, 0, 8))
        wj = hat(row(place, 1, 8), row(weight_ref, 1, 8))
        values = inc_ref[s]
        u = jnp.concatenate(
            [jnp.broadcast_to(values[f : f + 1], (8, C)) * wi for f in range(FIELDS)], 0
        )
        high, low = [], []
        for r in range(8):
            h, l = split(u * jnp.broadcast_to(wj[r : r + 1], (48, C)))
            high.append(h)
            low.append(l)
        high, low = jnp.concatenate(high, 0), jnp.concatenate(low, 0)
        z = row(weight_ref, 2, 16)
        z1h, z1l = split(z)
        z0h, z0l = split(1.0 - z)
        t = row(place, 2, 16)
        t0, t1 = as_bf(t), as_bf(t + 1)
        zero = jnp.zeros((16, C), BF)
        base = iota((16, C), 0)
        col_h, col_l = [], []
        for n in range(16):
            r = as_bf(base + 16 * n)
            first, second = r == t0, r == t1
            col_h.append(jnp.where(first, z0h, jnp.where(second, z1h, zero)))
            col_l.append(jnp.where(first, z0l, jnp.where(second, z1l, zero)))
        col_h, col_l = jnp.concatenate(col_h, 0), jnp.concatenate(col_l, 0)
        acc[...] += lax.dot_general(
            jnp.concatenate([high, high, low], 1),
            jnp.concatenate([col_h, col_l, col_h], 1),
            (((1,), (1,)), ((), ())),
            preferred_element_type=F32,
        )
        return carry

    lax.fori_loop(0, BLOCKS, source, 0)


def entries(shape, items):
    rows, cols = iota(shape, 0), iota(shape, 1)
    out = jnp.zeros(shape, F32)
    for r, c, value in items:
        out = jnp.where((rows == r) & (cols == c), value, out)
    return out


def prepare_i(ifac_ref, coup_ref, i_mat, i_state, i_ends, i_maps_own):
    n = FIELDS * CI
    r, c = iota((n, n), 0), iota((n, n), 1)
    same = (r >> 3) == (c >> 3)
    flip = jnp.where(same & ((r & 7) + (c & 7) == 7), 1.0, 0.0)
    spread = jnp.where(iota((CI, n), 0) == (iota((CI, n), 1) & 7), 1.0, 0.0)

    def diagonal(direction):
        flat = ifac_ref[direction].reshape(n, CI)
        return jnp.where(same, mm(flat, spread), 0.0)

    low = diagonal(0)
    up = mm(flip, mm(diagonal(1), flip))
    whole = mm(up, low)
    shape = (n, 24)
    e_low = entries(
        shape,
        [(8 * f, f, coup_ref[0, 0, f]) for f in range(FIELDS)]
        + [(8 * f, 6 + f, coup_ref[1, 0, f]) for f in range(FIELDS)]
        + [(8 * f + 1, f, coup_ref[2, 0, f]) for f in range(FIELDS)],
    )
    e_up = entries(
        shape,
        [(8 * f + 7, 12 + f, coup_ref[0, 1, f]) for f in range(FIELDS)]
        + [(8 * f + 7, 18 + f, coup_ref[1, 1, f]) for f in range(FIELDS)]
        + [(8 * f + 6, 12 + f, coup_ref[2, 1, f]) for f in range(FIELDS)],
    )
    infl_low = mm(low, e_low)
    state = -mm(up, infl_low + e_up)
    sel_shape = (24, n)
    comp = [(a, f) for a in range(2) for f in range(FIELDS)]
    sel_e = entries(sel_shape, [(a * 6 + f, 8 * f + 7 - a, 1.0) for a, f in comp])
    sel_p = entries(sel_shape, [(12 + a * 6 + f, 8 * f + a, 1.0) for a, f in comp])
    i_mat[...] = whole
    i_state[...] = state
    i_ends[...] = mm(sel_e, low) + mm(sel_p, whole)
    between = mm(sel_p, state) - mm(sel_e, infl_low)
    fold_r, fold_c = iota((24, CK), 0), iota((24, CK), 1)
    fold = jnp.where((fold_r >= 6 * fold_c) & (fold_r < 6 * fold_c + 6), 1.0, 0.0)
    i_maps_own[...] = mm(between, fold)


def prepare_k(kfac_ref, coup_ref, k_mat, k_state, k_ends, k_pad):
    n = CK
    flip = jnp.where(iota((n, n), 0) + iota((n, n), 1) == n - 1, 1.0, 0.0)
    sel_e = entries((8, n), [(0, n - 1, 1.0), (1, n - 2, 1.0)])
    sel_p = entries((8, n), [(2, 0, 1.0), (3, 1, 1.0)])

    def field(f, carry):
        low = kfac_ref[0, f]
        up = mm(flip, mm(kfac_ref[1, f], flip))
        whole = mm(up, low)
        e_low = entries(
            (8, n),
            [(0, 0, coup_ref[0, 2, f]), (0, 1, coup_ref[2, 2, f]), (1, 0, coup_ref[1, 2, f])],
        )
        e_up = entries(
            (8, n),
            [
                (2, n - 1, coup_ref[0, 3, f]),
                (2, n - 2, coup_ref[2, 3, f]),
                (3, n - 1, coup_ref[1, 3, f]),
            ],
        )
        infl_low = mm_nt(e_low, low)
        state = -mm_nt(infl_low + e_up, up)
        k_mat[f] = whole
        k_state[f] = state
        k_ends[f] = mm(sel_e, low) + mm(sel_p, whole)
        pad = jnp.zeros((n - 8, n), F32)
        k_pad[f] = mm_nt(sel_p, jnp.concatenate([pad, state], 0)) - mm_nt(
            sel_e, jnp.concatenate([pad, infl_low], 0)
        )
        return carry

    lax.fori_loop(0, FIELDS, field, 0)


def chain(count, ends, maps, keep):
    shape = ends(0)[0].shape
    s = [jnp.zeros(shape, F32)] * 2
    tops = []
    for n in range(count):
        e0, e1, p0, p1 = ends(n)
        m = maps(n)
        keep(n, 0, s)
        tops.append(
            [p0 + m[2][0] * s[0] + m[2][1] * s[1], p1 + m[3][0] * s[0] + m[3][1] * s[1]]
        )
        if n < count - 1:
            s = [e0 + m[0][0] * s[0] + m[0][1] * s[1], e1 + m[1][0] * s[0] + m[1][1] * s[1]]
    t = [jnp.zeros(shape, F32)] * 2
    for n in range(count - 1, -1, -1):
        m = maps(n)
        keep(n, 1, t)
        if n > 0:
            q0, q1 = tops[n]
            t = [q0 + m[2][2] * t[0] + m[2][3] * t[1], q1 + m[3][2] * t[0] + m[3][3] * t[1]]


def columns_of(block, first, width):
    def one(a, b):
        return jnp.broadcast_to(
            block[6 * a : 6 * a + 6, first + b : first + b + 1], (FIELDS, width)
        )

    return [
        [one(a, b) if a >= 2 or b < 2 else None for b in range(4)] for a in range(4)
    ]


def main_kernel(
    inc_ref,
    res_ref,
    ifac_ref,
    kfac_ref,
    coup_ref,
    cell_ref,
    weight_ref,
    out_ref,
    acc,
    place,
    x,
    i_mat,
    i_state,
    i_ends,
    i_maps,
    i_out,
    i_in,
    s_out,
    s_in,
    k_mat,
    k_state,
    k_ends,
    k_pad,
    k_all,
    k_st,
    xk,
    map_send,
    map_recv,
    end_send,
    end_recv,
    st_send,
    st_recv,
    k_send,
    k_recv,
):
    line, block = lax.axis_index("line"), lax.axis_index("block")
    barrier = pltpu.get_barrier_semaphore()
    for d in range(1, LINES):
        pl.semaphore_signal(
            barrier, inc=1, device_id={"line": (line + d) % LINES}, device_id_type=MESH
        )
    for d in range(1, BLOCKS):
        pl.semaphore_signal(
            barrier, inc=1, device_id={"block": (block + d) % BLOCKS}, device_id_type=MESH
        )
    prepare_i(ifac_ref, coup_ref, i_mat, i_state, i_ends, i_maps.at[line])
    pl.semaphore_wait(barrier, LINES + BLOCKS - 2)

    def to_line(d, src, dst, send, recv):
        return pltpu.make_async_remote_copy(
            src_ref=src,
            dst_ref=dst,
            send_sem=send.at[d],
            recv_sem=recv.at[d],
            device_id={"line": (line + d) % LINES},
            device_id_type=MESH,
        )

    map_copies = [
        to_line(d, i_maps.at[line], i_maps.at[line], map_send, map_recv) for d in range(1, LINES)
    ]
    for copy in map_copies:
        copy.start()
    prepare_k(kfac_ref, coup_ref, k_mat, k_state, k_ends, k_pad)
    scatter_all(inc_ref, cell_ref, weight_ref, acc, place)

    n = FIELDS * CI
    for j in range(CJ):
        total = res_ref[:, j].reshape(n, CK)
        if j < 8:
            total = total + acc[j * n : (j + 1) * n, 0:CK]
        if j >= 7:
            total = total + acc[(j - 7) * n : (j - 6) * n, CK : 2 * CK]
        x[:, j * CK : (j + 1) * CK] = total
    x[:, CJ * CK :] = jnp.zeros((n, CK), F32)

    ends = mm(i_ends[...], x[...])
    for c in range(LINES):
        i_out[c] = ends[:, c * 256 : (c + 1) * 256]
    i_in[line] = i_out[line]
    end_copies = [
        to_line(d, i_out.at[(line + d) % LINES], i_in.at[line], end_send, end_recv)
        for d in range(1, LINES)
    ]
    for copy in end_copies:
        copy.start()
    x[...] = mm(i_mat[...], x[...])
    for copy in map_copies:
        copy.wait()
    for copy in end_copies:
        copy.wait()

    def i_end(s):
        return [i_in[s, 6 * a : 6 * a + 6, :] for a in range(4)]

    i_cols = [columns_of(i_maps[s], 0, 256) for s in range(LINES)]

    def i_keep(s, up, state):
        for a in range(2):
            at = 12 * up + 6 * a
            s_out[s, at : at + 6, :] = state[a]

    chain(LINES, i_end, lambda s: i_cols[s], i_keep)
    s_in[line] = s_out[line]
    st_copies = [
        to_line(d, s_out.at[(line + d) % LINES], s_in.at[line], st_send, st_recv)
        for d in range(1, LINES)
    ]
    for copy in st_copies:
        copy.start()
    for copy in st_copies:
        copy.wait()
    for c in range(LINES):
        part = x[:, c * 256 : (c + 1) * 256] + mm(i_state[...], s_in[c])
        for jj in range(2):
            j = 2 * c + jj
            for f in range(FIELDS):
                xk[f, j * 8 : j * 8 + 8, :] = part[f * 8 : f * 8 + 8, jj * CK : (jj + 1) * CK]

    for f in range(FIELDS):
        found = mm_nt(k_ends[f], xk[f]) + k_pad[f]
        for a in range(4):
            k_all[block, 6 * a + f : 6 * a + f + 1, :] = found[a : a + 1]
    k_copies = [
        pltpu.make_async_remote_copy(
            src_ref=k_all.at[block],
            dst_ref=k_all.at[block],
            send_sem=k_send.at[d],
            recv_sem=k_recv.at[d],
            device_id={"block": (block + d) % BLOCKS},
            device_id_type=MESH,
        )
        for d in range(1, BLOCKS)
    ]
    for copy in k_copies:
        copy.start()
    for f in range(FIELDS):
        xk[f] = mm_nt(xk[f], k_mat[f])
    for copy in k_copies:
        copy.wait()

    def k_end(s):
        return [k_all[s, 6 * a : 6 * a + 6, :] for a in range(4)]

    k_cols = [columns_of(k_all[s], 120, CK) for s in range(BLOCKS)]
    kept = [[jnp.zeros((FIELDS, CK), F32)] * 2 for _ in range(2)]

    def k_keep(s, up, state):
        kept[up] = [jnp.where(block == s, state[a], kept[up][a]) for a in range(2)]

    chain(BLOCKS, k_end, lambda s: k_cols[s], k_keep)
    k_st[...] = jnp.zeros_like(k_st)
    for f in range(FIELDS):
        for a in range(4):
            k_st[f, a : a + 1, :] = kept[a // 2][a % 2][f : f + 1]
    for f in range(FIELDS):
        done = xk[f] + mm_tn(k_st[f], k_state[f])
        out_ref[f] = done[0 : CJ * CI].reshape(CJ, CI, CK)


def main(incoming, residual, i_factors, k_factors, couplings, donor_cell, donor_weight):
    vmem = pl.BlockSpec(memory_space=pltpu.VMEM)
    n = FIELDS * CI
    dma = pltpu.SemaphoreType.DMA
    return pl.pallas_call(
        main_kernel,
        out_shape=jax.ShapeDtypeStruct((FIELDS, CJ, CI, CK), F32),
        in_specs=[vmem] * 4 + [pl.BlockSpec(memory_space=pltpu.SMEM)] + [vmem] * 2,
        out_specs=vmem,
        scratch_shapes=[
            pltpu.VMEM((384, 256), F32),
            pltpu.VMEM((3, BLOCKS, CAP), jnp.int32),
            pltpu.VMEM((n, 16 * CK), F32),
            pltpu.VMEM((n, n), F32),
            pltpu.VMEM((n, 24), F32),
            pltpu.VMEM((24, n), F32),
            pltpu.VMEM((LINES, 24, CK), F32),
            pltpu.VMEM((LINES, 24, 256), F32),
            pltpu.VMEM((LINES, 24, 256), F32),
            pltpu.VMEM((LINES, 24, 256), F32),
            pltpu.VMEM((LINES, 24, 256), F32),
            pltpu.VMEM((FIELDS, CK, CK), F32),
            pltpu.VMEM((FIELDS, 8, CK), F32),
            pltpu.VMEM((FIELDS, 8, CK), F32),
            pltpu.VMEM((FIELDS, 8, CK), F32),
            pltpu.VMEM((BLOCKS, 24, CK), F32),
            pltpu.VMEM((FIELDS, 8, CK), F32),
            pltpu.VMEM((FIELDS, CK, CK), F32),
            dma((LINES,)),
            dma((LINES,)),
            dma((LINES,)),
            dma((LINES,)),
            dma((LINES,)),
            dma((LINES,)),
            dma((BLOCKS,)),
            dma((BLOCKS,)),
        ],
        compiler_params=pltpu.CompilerParams(
            vmem_limit_bytes=56 * 2**20, collective_id=0, has_side_effects=True
        ),
        name="main",
    )(incoming, residual, i_factors, k_factors, couplings, donor_cell, donor_weight)


def per_device(
    residual,
    adjoint,
    i_factors,
    k_factors,
    couplings,
    receptor_cell,
    send_count,
    donor_cell,
    donor_weight,
):
    outgoing = gather(adjoint.transpose(0, 2, 1, 3), receptor_cell[0, 0], send_count[0, 0])
    incoming = lax.all_to_all(outgoing, "block", split_axis=0, concat_axis=0, tiled=True)
    update = main(
        incoming,
        residual.transpose(0, 2, 1, 3),
        i_factors[0],
        k_factors[0],
        couplings[0, 0].transpose(1, 0, 2),
        donor_cell[0, 0],
        donor_weight[0, 0],
    )
    return update.transpose(0, 2, 1, 3)


def solution(mesh):
    return jax.shard_map(
        per_device,
        mesh=mesh,
        in_specs=(
            P(None, "line", None, "block"),
            P(None, "line", None, "block"),
            P("block", None, None, "line", None),
            P("line", None, None, "block", None),
            P("line", "block", None, None, None),
            P("line", "block", None, None),
            P("line", "block", None),
            P("line", "block", None, None),
            P("line", "block", None, None, None),
        ),
        out_specs=P(None, "line", None, "block"),
        check_vma=False,
    )
```

time: 1830 us -> 101 us (0.06)
  other arithmetic: 1500 us -> 0 us
  local copies, waits for them, and re-layouts: 161 us -> 1.75 us
  blocking collectives: 141 us -> 25.2 us
  Pallas kernels: 0 us -> 73.5 us
  matrix products: 20.2 us -> 0 us
    scatter-add x1 -> x0, other arithmetic: 1400 us -> none  [spread_donors(): return right_side.at[:, targets].add(spread)]
    all_gather x8 -> x0, blocking collectives: 141 us -> none  [carried_in(): everything = jax.tree.map(lambda part: lax.all_gather(part, axis), array)]
    gather x2 -> x0, local copies, waits for them, and re-layouts: 122 us -> none  [per_device(): jnp.take(flat_adjoint, receptor_index, axis=1)]
    mul x1 -> x0, other arithmetic: 88.5 us -> none  [spread_donors(): spread = jnp.tile(values, (1, 8)) * weights[None, :]]
    pallas_call x0 -> x2, Pallas kernels: none -> 73.5 us  [the longest x1 54.9 us: main(): pl.pallas_call(main_kernel, out_shape=jax.ShapeDtypeStruct((FIELDS, CJ, C...]
    all_to_all x0 -> x1, blocking collectives: none -> 25.2 us  [per_device(): lax.all_to_all(outgoing, 'block', split_axis=0, concat_axis=0, tiled=True)]
    dot_general x60 -> x0, matrix products: 20.2 us -> none  [the longest x48 13.2 us: compose(): jnp.einsum('fab,fbl->fal', next_map, first_vec, precision=lax.Precision.H...]
  transfers between devices with their start and end apart: 1 -> 0, of which waited for: 0 -> 0; matrix products, arithmetic and copies ran while one was open for 1% -> 0% of each run, Pallas kernels for 0% -> 0%
where the time goes in v1:
time: 101 us; the launch traced here: 100 us
  Pallas kernels  73.5 us (73%)
  blocking collectives  25.2 us (25%)
  local copies, waits for them, and re-layouts  1.75 us (2%)
    pallas_call x1, Pallas kernels, main(): pl.pallas_call(main_kernel, out_shape=jax.ShapeDtypeStruct((FIELDS, CJ, C...  54.9 us
    all_to_all x1, blocking collectives, per_device(): lax.all_to_all(outgoing, 'block', split_axis=0, concat_axis=0, tiled=True)  25.2 us
    pallas_call x1, Pallas kernels, gather(): pl.pallas_call(gather_kernel, out_shape=jax.ShapeDtypeStruct((BLOCKS, FIE...  18.6 us

profile of v1, /device:TPU:0, one launch (start us, length us, event | category | flops | bytes accessed | tf_op | source)
XLA Modules:
  0.0 100.5 jit_solution(12825262275398489771)
XLA Ops:
  0.0 18.6 %gather.1 = f32[16,6,2048]{2,1,0:T(8,128)} custom-call(f32[6,15,8,128]{3,2,1,0:T(8,128)} %bitcast.15, s32[16,2048]{1,0:T(8,128)} %bitcast.17, s32[16]{0:T(128)} %bitcast.21), custom_call_target="tpu_custom_call" | custom-call | tf_op jit(solution)/shard_map/gather/pallas_call | solution.py:87
  18.6 25.2 %all_to_all.5.inc_ref = f32[16,6,2048]{2,1,0:T(8,128)} all-to-all(f32[16,6,2048]{2,1,0:T(8,128)} %gather.1), channel_id=1, replica_groups=mesh['line'=8,'block'=16] {'block'}, dimensions={0} | all-to-all | bytes 1572864 | tf_op jit(solution)/shard_map/all_to_all | solution.py:493
  43.8 54.9 %main.1 = f32[6,15,8,128]{3,2,1,0:T(8,128)} custom-call(f32[16,6,2048]{2,1,0:T(8,128)} %all_to_all.5.inc_ref, f32[6,15,8,128]{3,2,1,0:T(8,128)} %bitcast.16, f32[2,6,8,8]{3,2,1,0:T(8,128)} %bitcast.19, f32[2,6,128,128]{3,2,1,0:T(8,128)} %bitcast.13, f32[3,4,6]{2,1,0:T(4,128)} %bitcast.20, s32[16,2048]{1,0:T(8,128)} %bitcast.18, f32[3,16,2048]{2,1,0:T(8,128)} %bitcast.14), custom_call_target="tpu_custom_call" | custom-call | tf_op jit(solution)/shard_map/main/pallas_call | solution.py:441
  98.7 1.7 %copy.11 = f32[6,8,15,128]{3,1,2,0:T(8,128)} copy(f32[6,8,15,128]{3,1,2,0:T(8,128)} %bitcast.12) | data formatting | bytes 737280

commit v2 on v1

--- a/solution.py
+++ b/solution.py
@@ -9,6 +9,9 @@
 
 F32, BF = jnp.float32, jnp.bfloat16
 FIELDS, CI, CJ, CK, CAP = 6, 8, 15, 128, 2048
+HEAD = 5 * CAP // 8
+REST = CAP - HEAD
+PART = 384 // 16
 LINES, BLOCKS = 8, 16
 HIGHEST = lax.Precision.HIGHEST
 MESH = pl.DeviceIdType.MESH
@@ -49,7 +52,7 @@
     return i, ij - i * CJ, cell & 127
 
 
-def gather_kernel(adj_ref, cell_ref, count_ref, out_ref, table, where_ref):
+def gather_table(adj_ref, table):
     for f in range(FIELDS):
         planes = [adj_ref[f, j] for j in range(CJ)] + [jnp.zeros((CI, CK), F32)]
         for half in range(2):
@@ -57,101 +60,70 @@
             row, col = f * 64, half * CK
             table[row : row + 64, col : col + CK] = high
             table[row : row + 64, 256 + col : 256 + col + CK] = low
-    i, j, k = cell_parts(cell_ref[...])
-    where_ref[0] = (j & 7) * CI + i
-    where_ref[1] = (j >> 3) * CK + k
-
-    def owner(s, carry):
-        C = CAP
-        group = jnp.broadcast_to(where_ref[0, pl.ds(s, 1), :], (64, C))
-        slot = as_bf(jnp.broadcast_to(where_ref[1, pl.ds(s, 1), :], (16, C)))
-        one, zero = jnp.ones((16, C), BF), jnp.zeros((16, C), BF)
-        base = iota((16, C), 0)
-        hot = [jnp.where(as_bf(base + 16 * n) == slot, one, zero) for n in range(16)]
-        hot = jnp.concatenate(hot, 0)
-        found = jnp.dot(
-            table[...], jnp.concatenate([hot, hot], 0), preferred_element_type=F32
-        ).reshape(FIELDS, 64, C)
-        mine = iota((64, C), 0) == group
-        live = iota((1, C), 1) < count_ref[s]
-        for f in range(FIELDS):
-            picked = jnp.sum(jnp.where(mine, found[f], 0.0), axis=0, keepdims=True)
-            out_ref[s, f : f + 1, :] = jnp.where(live, picked, 0.0)
-        return carry
-
-    lax.fori_loop(0, BLOCKS, owner, 0)
-
-
-def gather(adjoint, receptor_cell, send_count):
-    vmem = pl.BlockSpec(memory_space=pltpu.VMEM)
-    return pl.pallas_call(
-        gather_kernel,
-        out_shape=jax.ShapeDtypeStruct((BLOCKS, FIELDS, CAP), F32),
-        in_specs=[vmem, vmem, pl.BlockSpec(memory_space=pltpu.SMEM)],
-        out_specs=vmem,
-        scratch_shapes=[
-            pltpu.VMEM((FIELDS * 64, 512), BF),
-            pltpu.VMEM((2, BLOCKS, CAP), jnp.int32),
-        ],
-        compiler_params=pltpu.CompilerParams(vmem_limit_bytes=56 * 2**20),
-        name="gather",
-    )(adjoint, receptor_cell, send_count)
-
-
-def scatter_all(inc_ref, cell_ref, weight_ref, acc, place):
-    i, j, k = cell_parts(cell_ref[...])
+
+
+def gather_slots(table, group_row, slot_row):
+    C = group_row.shape[1]
+    slot = as_bf(jnp.broadcast_to(slot_row, (16, C)))
+    one, zero = jnp.ones((16, C), BF), jnp.zeros((16, C), BF)
+    base = iota((16, C), 0)
+    hot = [jnp.where(as_bf(base + 16 * n) == slot, one, zero) for n in range(16)]
+    hot = jnp.concatenate(hot, 0)
+    found = jnp.dot(
+        table[...], jnp.concatenate([hot, hot], 0), preferred_element_type=F32
+    ).reshape(FIELDS, 64, C)
+    mine = iota((64, C), 0) == jnp.broadcast_to(group_row, (64, C))
+    return [
+        jnp.sum(jnp.where(mine, found[f], 0.0), axis=0, keepdims=True) for f in range(FIELDS)
+    ]
+
+
+def scatter_slots(values, base_i, base_j, base_t, x, y, z):
+    C = x.shape[1]
+
+    def wide(row, n):
+        return jnp.broadcast_to(row, (n, C))
+
+    at = iota((8, C), 0)
+
+    def hat(base, t):
+        base, t = wide(base, 8), wide(t, 8)
+        return jnp.where(at == base, 1.0 - t, jnp.where(at == base + 1, t, 0.0))
+
+    wi, wj = hat(base_i, x), hat(base_j, y)
+    u = jnp.concatenate([wide(v, 8) * wi for v in values], 0)
+    high, low = [], []
+    for r in range(8):
+        h, l = split(u * wide(wj[r : r + 1], 48))
+        high.append(h)
+        low.append(l)
+    high, low = jnp.concatenate(high, 0), jnp.concatenate(low, 0)
+    z = wide(z, 16)
+    z1h, z1l = split(z)
+    z0h, z0l = split(1.0 - z)
+    t = wide(base_t, 16)
+    t0, t1 = as_bf(t), as_bf(t + 1)
+    zero = jnp.zeros((16, C), BF)
+    base = iota((16, C), 0)
+    col_h, col_l = [], []
+    for n in range(16):
+        r = as_bf(base + 16 * n)
+        first, second = r == t0, r == t1
+        col_h.append(jnp.where(first, z0h, jnp.where(second, z1h, zero)))
+        col_l.append(jnp.where(first, z0l, jnp.where(second, z1l, zero)))
+    col_h, col_l = jnp.concatenate(col_h, 0), jnp.concatenate(col_l, 0)
+    return lax.dot_general(
+        jnp.concatenate([high, high, low], 1),
+        jnp.concatenate([col_h, col_l, col_h], 1),
+        (((1,), (1,)), ((), ())),
+        preferred_element_type=F32,
+    )
+
+
+def donor_parts(cell):
+    i, j, k = cell_parts(cell)
     upper = jnp.where(j >= 7, 1, 0)
-    place[0] = i
-    place[1] = j - 7 * upper
-    place[2] = upper * CK + k
-    acc[...] = jnp.zeros_like(acc)
-
-    def source(s, carry):
-        C = CAP
-
-        def row(ref, a, n):
-            return jnp.broadcast_to(ref[a, pl.ds(s, 1), :], (n, C))
-
-        at = iota((8, C), 0)
-
-        def hat(base, t):
-            return jnp.where(at == base, 1.0 - t, jnp.where(at == base + 1, t, 0.0))
-
-        wi = hat(row(place, 0, 8), row(weight_ref, 0, 8))
-        wj = hat(row(place, 1, 8), row(weight_ref, 1, 8))
-        values = inc_ref[s]
-        u = jnp.concatenate(
-            [jnp.broadcast_to(values[f : f + 1], (8, C)) * wi for f in range(FIELDS)], 0
-        )
-        high, low = [], []
-        for r in range(8):
-            h, l = split(u * jnp.broadcast_to(wj[r : r + 1], (48, C)))
-            high.append(h)
-            low.append(l)
-        high, low = jnp.concatenate(high, 0), jnp.concatenate(low, 0)
-        z = row(weight_ref, 2, 16)
-        z1h, z1l = split(z)
-        z0h, z0l = split(1.0 - z)
-        t = row(place, 2, 16)
-        t0, t1 = as_bf(t), as_bf(t + 1)
-        zero = jnp.zeros((16, C), BF)
-        base = iota((16, C), 0)
-        col_h, col_l = [], []
-        for n in range(16):
-            r = as_bf(base + 16 * n)
-            first, second = r == t0, r == t1
-            col_h.append(jnp.where(first, z0h, jnp.where(second, z1h, zero)))
-            col_l.append(jnp.where(first, z0l, jnp.where(second, z1l, zero)))
-        col_h, col_l = jnp.concatenate(col_h, 0), jnp.concatenate(col_l, 0)
-        acc[...] += lax.dot_general(
-            jnp.concatenate([high, high, low], 1),
-            jnp.concatenate([col_h, col_l, col_h], 1),
-            (((1,), (1,)), ((), ())),
-            preferred_element_type=F32,
-        )
-        return carry
-
-    lax.fori_loop(0, BLOCKS, source, 0)
+    return i, j - 7 * upper, upper * CK + k
 
 
 def entries(shape, items):
@@ -204,16 +176,38 @@
     i_maps_own[...] = mm(between, fold)
 
 
-def prepare_k(kfac_ref, coup_ref, k_mat, k_state, k_ends, k_pad):
+def stack3(x, axis, middle_low):
+    high, low = split(x)
+    return jnp.concatenate([high, low, high] if middle_low else [high, high, low], axis)
+
+
+def mm3(a, b):
+    return jnp.dot(stack3(a, 1, False), stack3(b, 0, True), preferred_element_type=F32)
+
+
+def nt(a, b):
+    return lax.dot_general(a, b, (((1,), (1,)), ((), ())), preferred_element_type=F32)
+
+
+def mm3_nt(a, b):
+    return nt(stack3(a, 1, False), stack3(b, 1, True))
+
+
+def prepare_k(fields, kfac_ref, coup_ref, k_mat, k_state, k_ends, k_pad):
     n = CK
-    flip = jnp.where(iota((n, n), 0) + iota((n, n), 1) == n - 1, 1.0, 0.0)
+    flip = jnp.where(iota((n, n), 0) + iota((n, n), 1) == n - 1, 1.0, 0.0).astype(BF)
+    flip_cols = jnp.concatenate([flip, flip], 0)
+    flip_rows = jnp.concatenate([flip, flip], 1)
     sel_e = entries((8, n), [(0, n - 1, 1.0), (1, n - 2, 1.0)])
     sel_p = entries((8, n), [(2, 0, 1.0), (3, 1, 1.0)])
-
-    def field(f, carry):
+    pad = jnp.zeros((n - 8, n), F32)
+    for f in fields:
         low = kfac_ref[0, f]
-        up = mm(flip, mm(kfac_ref[1, f], flip))
-        whole = mm(up, low)
+        up = jnp.dot(
+            jnp.concatenate(split(kfac_ref[1, f]), 1), flip_cols, preferred_element_type=F32
+        )
+        up = jnp.dot(flip_rows, jnp.concatenate(split(up), 0), preferred_element_type=F32)
+        whole = mm3(up, low)
         e_low = entries(
             (8, n),
             [(0, 0, coup_ref[0, 2, f]), (0, 1, coup_ref[2, 2, f]), (1, 0, coup_ref[1, 2, f])],
@@ -226,18 +220,16 @@
                 (3, n - 1, coup_ref[1, 3, f]),
             ],
         )
-        infl_low = mm_nt(e_low, low)
-        state = -mm_nt(infl_low + e_up, up)
-        k_mat[f] = whole
+        infl_low = mm3_nt(e_low, low)
+        state = -mm3_nt(infl_low + e_up, up)
+        k_mat[f] = stack3(whole, 1, True)
         k_state[f] = state
-        k_ends[f] = mm(sel_e, low) + mm(sel_p, whole)
-        pad = jnp.zeros((n - 8, n), F32)
-        k_pad[f] = mm_nt(sel_p, jnp.concatenate([pad, state], 0)) - mm_nt(
+        k_ends[f] = stack3(
+            jnp.concatenate([low[n - 1 : n], low[n - 2 : n - 1], whole[0:2], pad[0:4]], 0), 1, False
+        )
+        k_pad[f] = mm3_nt(sel_p, jnp.concatenate([pad, state], 0)) - mm3_nt(
             sel_e, jnp.concatenate([pad, infl_low], 0)
         )
-        return carry
-
-    lax.fori_loop(0, FIELDS, field, 0)
 
 
 def chain(count, ends, maps, keep):
@@ -274,16 +266,27 @@
 
 
 def main_kernel(
-    inc_ref,
+    adj_ref,
+    rec_ref,
     res_ref,
     ifac_ref,
     kfac_ref,
     coup_ref,
+    count_ref,
     cell_ref,
     weight_ref,
     out_ref,
+    table,
+    where_ref,
+    place,
+    outgoing,
+    incoming,
+    info_out,
+    info_in,
     acc,
-    place,
+    acc_rest,
+    rs_in,
+    ag_in,
     x,
     i_mat,
     i_state,
@@ -300,6 +303,14 @@
     k_all,
     k_st,
     xk,
+    info_send,
+    info_recv,
+    a2a_send,
+    a2a_recv,
+    rs_send,
+    rs_recv,
+    ag_send,
+    ag_recv,
     map_send,
     map_recv,
     end_send,
@@ -313,14 +324,12 @@
     barrier = pltpu.get_barrier_semaphore()
     for d in range(1, LINES):
         pl.semaphore_signal(
-            barrier, inc=1, device_id={"line": (line + d) % LINES}, device_id_type=MESH
+            barrier, inc=1, device_id={"line": lax.rem(line + d, LINES)}, device_id_type=MESH
         )
     for d in range(1, BLOCKS):
         pl.semaphore_signal(
-            barrier, inc=1, device_id={"block": (block + d) % BLOCKS}, device_id_type=MESH
-        )
-    prepare_i(ifac_ref, coup_ref, i_mat, i_state, i_ends, i_maps.at[line])
-    pl.semaphore_wait(barrier, LINES + BLOCKS - 2)
+            barrier, inc=1, device_id={"block": lax.rem(block + d, BLOCKS)}, device_id_type=MESH
+        )
 
     def to_line(d, src, dst, send, recv):
         return pltpu.make_async_remote_copy(
@@ -328,25 +337,142 @@
             dst_ref=dst,
             send_sem=send.at[d],
             recv_sem=recv.at[d],
-            device_id={"line": (line + d) % LINES},
+            device_id={"line": lax.rem(line + d, LINES)},
             device_id_type=MESH,
         )
 
+    def to_block(d, src, dst, send, recv):
+        return pltpu.make_async_remote_copy(
+            src_ref=src,
+            dst_ref=dst,
+            send_sem=send.at[d],
+            recv_sem=recv.at[d],
+            device_id={"block": lax.rem(block + d, BLOCKS)},
+            device_id_type=MESH,
+        )
+
+    def peer(d):
+        return lax.rem(block + d, BLOCKS)
+
+    def info_copy(d):
+        return to_block(d, info_out.at[peer(d)], info_in.at[block], info_send, info_recv)
+
+    def slot_copy(d):
+        return to_block(d, outgoing.at[peer(d)], incoming.at[block], a2a_send, a2a_recv)
+
+    def rs_copy(d):
+        return to_block(d, acc_rest.at[peer(d)], rs_in.at[block], rs_send, rs_recv)
+
+    def ag_copy(d):
+        return to_block(d, ag_in.at[block], ag_in.at[block], ag_send, ag_recv)
+
+    def over_peers(action):
+        def step(d, carry):
+            action(d)
+            return carry
+
+        lax.fori_loop(1, BLOCKS, step, 0)
+
+    hot = jnp.int32(0)
+    for o in range(BLOCKS):
+        hot = jnp.where(count_ref[o] == CAP, o, hot)
+
+    for p in range(BLOCKS):
+        info_out[p, 0:1, :] = cell_ref[p : p + 1, HEAD:].astype(F32)
+        for a in range(3):
+            info_out[p, a + 1 : a + 2, :] = weight_ref[a, p : p + 1, HEAD:]
+    gather_table(adj_ref, table)
+    i, j, k = cell_parts(rec_ref[...])
+    where_ref[0] = (j & 7) * CI + i
+    where_ref[1] = (j >> 3) * CK + k
+    for a, part in enumerate(donor_parts(cell_ref[...])):
+        place[a] = part
+    prepare_i(ifac_ref, coup_ref, i_mat, i_state, i_ends, i_maps.at[line])
+    pl.semaphore_wait(barrier, LINES + BLOCKS - 2)
+    over_peers(lambda d: info_copy(d).start())
+    info_in[block] = info_out[block]
+
+    def owner_step(d, carry):
+        o = peer(d)
+        rows = gather_slots(
+            table, where_ref[0, pl.ds(o, 1), 0:HEAD], where_ref[1, pl.ds(o, 1), 0:HEAD]
+        )
+        live = iota((1, HEAD), 1) < count_ref[o]
+        for f in range(FIELDS):
+            outgoing[o, f : f + 1, :] = jnp.where(live, rows[f], 0.0)
+
+        @pl.when(d < BLOCKS)
+        def _():
+            slot_copy(d).start()
+
+        return carry
+
+    lax.fori_loop(1, BLOCKS + 1, owner_step, 0)
+    incoming[block] = outgoing[block]
     map_copies = [
         to_line(d, i_maps.at[line], i_maps.at[line], map_send, map_recv) for d in range(1, LINES)
     ]
     for copy in map_copies:
         copy.start()
-    prepare_k(kfac_ref, coup_ref, k_mat, k_state, k_ends, k_pad)
-    scatter_all(inc_ref, cell_ref, weight_ref, acc, place)
+
+    over_peers(lambda d: info_copy(d).wait())
+    rest = gather_slots(
+        table, where_ref[0, pl.ds(hot, 1), HEAD:], where_ref[1, pl.ds(hot, 1), HEAD:]
+    )
+    info = info_in[hot]
+    found = scatter_slots(
+        rest,
+        *donor_parts(info[0:1].astype(jnp.int32)),
+        info[1:2],
+        info[2:3],
+        info[3:4],
+    )
+    for p in range(BLOCKS):
+        acc_rest[p] = found[p * PART : (p + 1) * PART]
+    rs_in[block] = acc_rest[block]
+    over_peers(lambda d: rs_copy(d).start())
+
+    acc[...] = jnp.zeros_like(acc)
+
+    def source_step(d, carry):
+        s = lax.rem(block + BLOCKS - d, BLOCKS)
+
+        @pl.when(d > 0)
+        def _():
+            slot_copy(d).wait_recv()
+
+        @pl.when(d == BLOCKS // 2)
+        def _():
+            over_peers(lambda e: rs_copy(e).wait())
+            total = rs_in[0]
+            for p in range(1, BLOCKS):
+                total = total + rs_in[p]
+            ag_in[block] = total
+            over_peers(lambda e: ag_copy(e).start())
+
+        def row(ref, a):
+            return ref[a, pl.ds(s, 1), 0:HEAD]
+
+        values = incoming[s]
+        acc[...] += scatter_slots(
+            [values[f : f + 1] for f in range(FIELDS)],
+            *[row(place, a) for a in range(3)],
+            *[row(weight_ref, a) for a in range(3)],
+        )
+        return carry
+
+    lax.fori_loop(0, BLOCKS, source_step, 0)
+    over_peers(lambda d: slot_copy(d).wait_send())
+    over_peers(lambda d: ag_copy(d).wait())
 
     n = FIELDS * CI
     for j in range(CJ):
         total = res_ref[:, j].reshape(n, CK)
-        if j < 8:
-            total = total + acc[j * n : (j + 1) * n, 0:CK]
-        if j >= 7:
-            total = total + acc[(j - 7) * n : (j - 6) * n, CK : 2 * CK]
+        for r, c in ((j, 0), (j - 7, CK)):
+            if 0 <= r < 8:
+                more = jnp.concatenate([ag_in[2 * r, :, c : c + CK], ag_in[2 * r + 1, :, c : c + CK]], 0)
+                more = jnp.where(hot == block, more, 0.0)
+                total = total + acc[r * n : (r + 1) * n, c : c + CK] + more
         x[:, j * CK : (j + 1) * CK] = total
     x[:, CJ * CK :] = jnp.zeros((n, CK), F32)
 
@@ -361,6 +487,8 @@
     for copy in end_copies:
         copy.start()
     x[...] = mm(i_mat[...], x[...])
+    k_refs = (kfac_ref, coup_ref, k_mat, k_state, k_ends, k_pad)
+    prepare_k(range(0, 3), *k_refs)
     for copy in map_copies:
         copy.wait()
     for copy in end_copies:
@@ -384,6 +512,7 @@
     ]
     for copy in st_copies:
         copy.start()
+    prepare_k(range(3, 6), *k_refs)
     for copy in st_copies:
         copy.wait()
     for c in range(LINES):
@@ -394,7 +523,7 @@
                 xk[f, j * 8 : j * 8 + 8, :] = part[f * 8 : f * 8 + 8, jj * CK : (jj + 1) * CK]
 
     for f in range(FIELDS):
-        found = mm_nt(k_ends[f], xk[f]) + k_pad[f]
+        found = nt(k_ends[f], stack3(xk[f], 1, True)) + k_pad[f]
         for a in range(4):
             k_all[block, 6 * a + f : 6 * a + f + 1, :] = found[a : a + 1]
     k_copies = [
@@ -411,7 +540,7 @@
     for copy in k_copies:
         copy.start()
     for f in range(FIELDS):
-        xk[f] = mm_nt(xk[f], k_mat[f])
+        xk[f] = nt(stack3(xk[f], 1, False), k_mat[f])
     for copy in k_copies:
         copy.wait()
 
@@ -434,18 +563,37 @@
         out_ref[f] = done[0 : CJ * CI].reshape(CJ, CI, CK)
 
 
-def main(incoming, residual, i_factors, k_factors, couplings, donor_cell, donor_weight):
-    vmem = pl.BlockSpec(memory_space=pltpu.VMEM)
+def sweep(
+    adjoint,
+    receptor_cell,
+    residual,
+    i_factors,
+    k_factors,
+    couplings,
+    send_count,
+    donor_cell,
+    donor_weight,
+):
+    vmem, smem = pl.BlockSpec(memory_space=pltpu.VMEM), pl.BlockSpec(memory_space=pltpu.SMEM)
     n = FIELDS * CI
     dma = pltpu.SemaphoreType.DMA
     return pl.pallas_call(
         main_kernel,
         out_shape=jax.ShapeDtypeStruct((FIELDS, CJ, CI, CK), F32),
-        in_specs=[vmem] * 4 + [pl.BlockSpec(memory_space=pltpu.SMEM)] + [vmem] * 2,
+        in_specs=[vmem] * 5 + [smem] * 2 + [vmem] * 2,
         out_specs=vmem,
         scratch_shapes=[
+            pltpu.VMEM((FIELDS * 64, 512), BF),
+            pltpu.VMEM((2, BLOCKS, CAP), jnp.int32),
+            pltpu.VMEM((3, BLOCKS, CAP), jnp.int32),
+            pltpu.VMEM((BLOCKS, FIELDS, HEAD), F32),
+            pltpu.VMEM((BLOCKS, FIELDS, HEAD), F32),
+            pltpu.VMEM((BLOCKS, 4, REST), F32),
+            pltpu.VMEM((BLOCKS, 4, REST), F32),
             pltpu.VMEM((384, 256), F32),
-            pltpu.VMEM((3, BLOCKS, CAP), jnp.int32),
+            pltpu.VMEM((BLOCKS, PART, 256), F32),
+            pltpu.VMEM((BLOCKS, PART, 256), F32),
+            pltpu.VMEM((BLOCKS, PART, 256), F32),
             pltpu.VMEM((n, 16 * CK), F32),
             pltpu.VMEM((n, n), F32),
             pltpu.VMEM((n, 24), F32),
@@ -455,27 +603,32 @@
             pltpu.VMEM((LINES, 24, 256), F32),
             pltpu.VMEM((LINES, 24, 256), F32),
             pltpu.VMEM((LINES, 24, 256), F32),
-            pltpu.VMEM((FIELDS, CK, CK), F32),
+            pltpu.VMEM((FIELDS, CK, 3 * CK), BF),
             pltpu.VMEM((FIELDS, 8, CK), F32),
-            pltpu.VMEM((FIELDS, 8, CK), F32),
+            pltpu.VMEM((FIELDS, 8, 3 * CK), BF),
             pltpu.VMEM((FIELDS, 8, CK), F32),
             pltpu.VMEM((BLOCKS, 24, CK), F32),
             pltpu.VMEM((FIELDS, 8, CK), F32),
             pltpu.VMEM((FIELDS, CK, CK), F32),
-            dma((LINES,)),
-            dma((LINES,)),
-            dma((LINES,)),
-            dma((LINES,)),
-            dma((LINES,)),
-            dma((LINES,)),
-            dma((BLOCKS,)),
-            dma((BLOCKS,)),
-        ],
+        ]
+        + [dma((BLOCKS,))] * 8
+        + [dma((LINES,))] * 6
+        + [dma((BLOCKS,))] * 2,
         compiler_params=pltpu.CompilerParams(
             vmem_limit_bytes=56 * 2**20, collective_id=0, has_side_effects=True
         ),
-        name="main",
-    )(incoming, residual, i_factors, k_factors, couplings, donor_cell, donor_weight)
+        name="sweep",
+    )(
+        adjoint,
+        receptor_cell,
+        residual,
+        i_factors,
+        k_factors,
+        couplings,
+        send_count,
+        donor_cell,
+        donor_weight,
+    )
 
 
 def per_device(
@@ -489,14 +642,14 @@
     donor_cell,
     donor_weight,
 ):
-    outgoing = gather(adjoint.transpose(0, 2, 1, 3), receptor_cell[0, 0], send_count[0, 0])
-    incoming = lax.all_to_all(outgoing, "block", split_axis=0, concat_axis=0, tiled=True)
-    update = main(
-        incoming,
+    update = sweep(
+        adjoint.transpose(0, 2, 1, 3),
+        receptor_cell[0, 0],
         residual.transpose(0, 2, 1, 3),
         i_factors[0],
         k_factors[0],
         couplings[0, 0].transpose(1, 0, 2),
+        send_count[0, 0],
         donor_cell[0, 0],
         donor_weight[0, 0],
     )

time: 101 us -> 59.4 us (0.59)
  blocking collectives: 25.2 us -> 0 us
  Pallas kernels: 73.5 us -> 57.5 us
    all_to_all x1 -> x0, blocking collectives: 25.2 us -> none  [per_device(): lax.all_to_all(outgoing, 'block', split_axis=0, concat_axis=0, tiled=True)]
    pallas_call x2 -> x1, Pallas kernels: 73.5 us -> 57.5 us  [sweep(): pl.pallas_call(main_kernel, out_shape=jax.ShapeDtypeStruct((FIELDS, CJ, C...]
where the time goes in v2:
time: 59.4 us; the launch traced here: 59.3 us
  Pallas kernels  57.5 us (97%)
  local copies, waits for them, and re-layouts  1.75 us (3%)
    pallas_call x1, Pallas kernels, sweep(): pl.pallas_call(main_kernel, out_shape=jax.ShapeDtypeStruct((FIELDS, CJ, C...  57.5 us
    unnamed x1, local copies, waits for them, and re-layouts  1.75 us

profile of v2, /device:TPU:0, one launch (start us, length us, event | category | flops | bytes accessed | tf_op | source)
XLA Modules:
  0.0 59.3 jit_solution(15068252082247964913)
XLA Ops:
  0.0 57.5 %sweep.1 = f32[6,15,8,128]{3,2,1,0:T(8,128)} custom-call(f32[6,15,8,128]{3,2,1,0:T(8,128)} %bitcast.15, s32[16,2048]{1,0:T(8,128)} %bitcast.17, f32[6,15,8,128]{3,2,1,0:T(8,128)} %bitcast.16, f32[2,6,8,8]{3,2,1,0:T(8,128)} %bitcast.19, f32[2,6,128,128]{3,2,1,0:T(8,128)} %bitcast.13, f32[3,4,6]{2,1,0:T(4,128)} %bitcast.20, s32[16]{0:T(128)} %bitcast.21, ...), custom_call_target="tpu_custom_call" | custom-call | tf_op jit(solution)/shard_map/sweep/pallas_call | solution.py:580
  57.5 1.7 %copy.11 = f32[6,8,15,128]{3,1,2,0:T(8,128)} copy(f32[6,8,15,128]{3,1,2,0:T(8,128)} %bitcast.12) | data formatting | bytes 737280

commit v3 on v2

--- a/solution.py
+++ b/solution.py
@@ -12,6 +12,8 @@
 HEAD = 5 * CAP // 8
 REST = CAP - HEAD
 PART = 384 // 16
+PIECES = HEAD // 256
+EARLY = 1
 LINES, BLOCKS = 8, 16
 HIGHEST = lax.Precision.HIGHEST
 MESH = pl.DeviceIdType.MESH
@@ -268,9 +270,9 @@
 def main_kernel(
     adj_ref,
     rec_ref,
-    res_ref,
+    res_hbm,
     ifac_ref,
-    kfac_ref,
+    kfac_hbm,
     coup_ref,
     count_ref,
     cell_ref,
@@ -283,6 +285,7 @@
     incoming,
     info_out,
     info_in,
+    rest,
     acc,
     acc_rest,
     rs_in,
@@ -319,7 +322,14 @@
     st_recv,
     k_send,
     k_recv,
+    res_ref,
+    kfac_ref,
+    load_sem,
 ):
+    load_res = pltpu.make_async_copy(res_hbm, res_ref, load_sem.at[0])
+    load_kfac = pltpu.make_async_copy(kfac_hbm, kfac_ref, load_sem.at[1])
+    load_res.start()
+    load_kfac.start()
     line, block = lax.axis_index("line"), lax.axis_index("block")
     barrier = pltpu.get_barrier_semaphore()
     for d in range(1, LINES):
@@ -388,40 +398,58 @@
     for a, part in enumerate(donor_parts(cell_ref[...])):
         place[a] = part
     prepare_i(ifac_ref, coup_ref, i_mat, i_state, i_ends, i_maps.at[line])
+    outgoing[:, FIELDS * PIECES :, :] = jnp.zeros((BLOCKS, 32 - FIELDS * PIECES, 256), F32)
+
+    def owner_step(t, carry):
+        owners = [peer(2 * t), peer(2 * t + 1)]
+        group_row, slot_row = [
+            jnp.concatenate([where_ref[a, pl.ds(o, 1), 0:HEAD] for o in owners], 1)
+            for a in range(2)
+        ]
+        rows = gather_slots(table, group_row, slot_row)
+        for n, o in enumerate(owners):
+            live = iota((1, HEAD), 1) < count_ref[o]
+            for f in range(FIELDS):
+                row = jnp.where(live, rows[f][:, n * HEAD : (n + 1) * HEAD], 0.0)
+                for q in range(PIECES):
+                    at = q * FIELDS + f
+                    outgoing[o, at : at + 1, :] = row[:, q * 256 : (q + 1) * 256]
+        return carry
+
+    lax.fori_loop(0, EARLY, owner_step, 0)
+    incoming[block] = outgoing[block]
+    for f, row in enumerate(
+        gather_slots(table, where_ref[0, pl.ds(hot, 1), HEAD:], where_ref[1, pl.ds(hot, 1), HEAD:])
+    ):
+        rest[f : f + 1, :] = row
+
     pl.semaphore_wait(barrier, LINES + BLOCKS - 2)
     over_peers(lambda d: info_copy(d).start())
-    info_in[block] = info_out[block]
-
-    def owner_step(d, carry):
-        o = peer(d)
-        rows = gather_slots(
-            table, where_ref[0, pl.ds(o, 1), 0:HEAD], where_ref[1, pl.ds(o, 1), 0:HEAD]
-        )
-        live = iota((1, HEAD), 1) < count_ref[o]
-        for f in range(FIELDS):
-            outgoing[o, f : f + 1, :] = jnp.where(live, rows[f], 0.0)
-
-        @pl.when(d < BLOCKS)
-        def _():
-            slot_copy(d).start()
-
+
+    def early_step(d, carry):
+        slot_copy(d).start()
         return carry
 
-    lax.fori_loop(1, BLOCKS + 1, owner_step, 0)
-    incoming[block] = outgoing[block]
+    lax.fori_loop(1, 2 * EARLY, early_step, 0)
     map_copies = [
         to_line(d, i_maps.at[line], i_maps.at[line], map_send, map_recv) for d in range(1, LINES)
     ]
     for copy in map_copies:
         copy.start()
+    info_in[block] = info_out[block]
+
+    def late_step(d, carry):
+        owner_step(d, carry)
+        slot_copy(2 * d).start()
+        slot_copy(2 * d + 1).start()
+        return carry
+
+    lax.fori_loop(EARLY, BLOCKS // 2, late_step, 0)
 
     over_peers(lambda d: info_copy(d).wait())
-    rest = gather_slots(
-        table, where_ref[0, pl.ds(hot, 1), HEAD:], where_ref[1, pl.ds(hot, 1), HEAD:]
-    )
     info = info_in[hot]
     found = scatter_slots(
-        rest,
+        [rest[f : f + 1, :] for f in range(FIELDS)],
         *donor_parts(info[0:1].astype(jnp.int32)),
         info[1:2],
         info[2:3],
@@ -434,14 +462,16 @@
 
     acc[...] = jnp.zeros_like(acc)
 
-    def source_step(d, carry):
-        s = lax.rem(block + BLOCKS - d, BLOCKS)
-
-        @pl.when(d > 0)
+    def source_step(t, carry):
+        sources = [lax.rem(block + BLOCKS - 2 * t - n, BLOCKS) for n in range(2)]
+
+        @pl.when(t > 0)
         def _():
-            slot_copy(d).wait_recv()
-
-        @pl.when(d == BLOCKS // 2)
+            slot_copy(2 * t).wait_recv()
+
+        slot_copy(2 * t + 1).wait_recv()
+
+        @pl.when(t == BLOCKS // 4)
         def _():
             over_peers(lambda e: rs_copy(e).wait())
             total = rs_in[0]
@@ -451,20 +481,28 @@
             over_peers(lambda e: ag_copy(e).start())
 
         def row(ref, a):
-            return ref[a, pl.ds(s, 1), 0:HEAD]
-
-        values = incoming[s]
+            return jnp.concatenate([ref[a, pl.ds(s, 1), 0:HEAD] for s in sources], 1)
+
+        values = [incoming[s] for s in sources]
         acc[...] += scatter_slots(
-            [values[f : f + 1] for f in range(FIELDS)],
+            [
+                jnp.concatenate(
+                    [v[q * FIELDS + f : q * FIELDS + f + 1] for v in values for q in range(PIECES)],
+                    1,
+                )
+                for f in range(FIELDS)
+            ],
             *[row(place, a) for a in range(3)],
             *[row(weight_ref, a) for a in range(3)],
         )
         return carry
 
-    lax.fori_loop(0, BLOCKS, source_step, 0)
+    lax.fori_loop(0, BLOCKS // 2, source_step, 0)
     over_peers(lambda d: slot_copy(d).wait_send())
     over_peers(lambda d: ag_copy(d).wait())
 
+    load_res.wait()
+    load_kfac.wait()
     n = FIELDS * CI
     for j in range(CJ):
         total = res_ref[:, j].reshape(n, CK)
@@ -575,21 +613,23 @@
     donor_weight,
 ):
     vmem, smem = pl.BlockSpec(memory_space=pltpu.VMEM), pl.BlockSpec(memory_space=pltpu.SMEM)
+    hbm = pl.BlockSpec(memory_space=pl.ANY)
     n = FIELDS * CI
     dma = pltpu.SemaphoreType.DMA
     return pl.pallas_call(
         main_kernel,
         out_shape=jax.ShapeDtypeStruct((FIELDS, CJ, CI, CK), F32),
-        in_specs=[vmem] * 5 + [smem] * 2 + [vmem] * 2,
+        in_specs=[vmem] * 2 + [hbm, vmem, hbm, smem, smem] + [vmem] * 2,
         out_specs=vmem,
         scratch_shapes=[
             pltpu.VMEM((FIELDS * 64, 512), BF),
             pltpu.VMEM((2, BLOCKS, CAP), jnp.int32),
             pltpu.VMEM((3, BLOCKS, CAP), jnp.int32),
-            pltpu.VMEM((BLOCKS, FIELDS, HEAD), F32),
-            pltpu.VMEM((BLOCKS, FIELDS, HEAD), F32),
+            pltpu.VMEM((BLOCKS, 32, 256), F32),
+            pltpu.VMEM((BLOCKS, 32, 256), F32),
             pltpu.VMEM((BLOCKS, 4, REST), F32),
             pltpu.VMEM((BLOCKS, 4, REST), F32),
+            pltpu.VMEM((FIELDS, REST), F32),
             pltpu.VMEM((384, 256), F32),
             pltpu.VMEM((BLOCKS, PART, 256), F32),
             pltpu.VMEM((BLOCKS, PART, 256), F32),
@@ -613,7 +653,12 @@
         ]
         + [dma((BLOCKS,))] * 8
         + [dma((LINES,))] * 6
-        + [dma((BLOCKS,))] * 2,
+        + [dma((BLOCKS,))] * 2
+        + [
+            pltpu.VMEM((FIELDS, CJ, CI, CK), F32),
+            pltpu.VMEM((2, FIELDS, CK, CK), F32),
+            dma((2,)),
+        ],
         compiler_params=pltpu.CompilerParams(
             vmem_limit_bytes=56 * 2**20, collective_id=0, has_side_effects=True
         ),

time: 59.4 us -> 54.5 us (0.918)
  Pallas kernels: 57.5 us -> 52.5 us
    pallas_call x1, Pallas kernels: 57.5 us -> 52.5 us  [sweep(): pl.pallas_call(main_kernel, out_shape=jax.ShapeDtypeStruct((FIELDS, CJ, C...]
where the time goes in v3:
time: 54.5 us; the launch traced here: 54.3 us
  Pallas kernels  52.5 us (96%)
  local copies, waits for them, and re-layouts  1.75 us (3%)
    pallas_call x1, Pallas kernels, sweep(): pl.pallas_call(main_kernel, out_shape=jax.ShapeDtypeStruct((FIELDS, CJ, C...  52.5 us
    unnamed x1, local copies, waits for them, and re-layouts  1.75 us

profile of v3, /device:TPU:0, one launch (start us, length us, event | category | flops | bytes accessed | tf_op | source)
XLA Modules:
  0.0 54.3 jit_solution(18443214294726260403)
XLA Ops:
  0.0 52.5 %sweep.1 = f32[6,15,8,128]{3,2,1,0:T(8,128)} custom-call(f32[6,15,8,128]{3,2,1,0:T(8,128)} %bitcast.15, s32[16,2048]{1,0:T(8,128)} %bitcast.17, f32[6,15,8,128]{3,2,1,0:T(8,128)} %bitcast.16, f32[2,6,8,8]{3,2,1,0:T(8,128)} %bitcast.19, f32[2,6,128,128]{3,2,1,0:T(8,128)} %bitcast.13, f32[3,4,6]{2,1,0:T(4,128)} %bitcast.20, s32[16]{0:T(128)} %bitcast.21, ...), custom_call_target="tpu_custom_call" | custom-call | tf_op jit(solution)/shard_map/sweep/pallas_call | solution.py:619
  52.5 1.7 %copy.11 = f32[6,8,15,128]{3,1,2,0:T(8,128)} copy(f32[6,8,15,128]{3,1,2,0:T(8,128)} %bitcast.12) | data formatting | bytes 737280

commit v4 on v3

--- a/solution.py
+++ b/solution.py
@@ -12,8 +12,13 @@
 HEAD = 5 * CAP // 8
 REST = CAP - HEAD
 PART = 384 // 16
+DIRECT = 2
+TABLED = FIELDS - DIRECT
+TOGETHER = 4
 PIECES = HEAD // 256
 EARLY = 1
+REST_AT = 0
+GRID_AT = 2
 LINES, BLOCKS = 8, 16
 HIGHEST = lax.Precision.HIGHEST
 MESH = pl.DeviceIdType.MESH
@@ -55,7 +60,7 @@
 
 
 def gather_table(adj_ref, table):
-    for f in range(FIELDS):
+    for f in range(TABLED):
         planes = [adj_ref[f, j] for j in range(CJ)] + [jnp.zeros((CI, CK), F32)]
         for half in range(2):
             high, low = split(jnp.concatenate(planes[8 * half : 8 * half + 8], 0))
@@ -64,7 +69,7 @@
             table[row : row + 64, 256 + col : 256 + col + CK] = low
 
 
-def gather_slots(table, group_row, slot_row):
+def gather_slots(adj_ref, table, group_row, slot_row):
     C = group_row.shape[1]
     slot = as_bf(jnp.broadcast_to(slot_row, (16, C)))
     one, zero = jnp.ones((16, C), BF), jnp.zeros((16, C), BF)
@@ -73,11 +78,29 @@
     hot = jnp.concatenate(hot, 0)
     found = jnp.dot(
         table[...], jnp.concatenate([hot, hot], 0), preferred_element_type=F32
-    ).reshape(FIELDS, 64, C)
+    ).reshape(TABLED, 64, C)
     mine = iota((64, C), 0) == jnp.broadcast_to(group_row, (64, C))
-    return [
-        jnp.sum(jnp.where(mine, found[f], 0.0), axis=0, keepdims=True) for f in range(FIELDS)
+    rows = [
+        jnp.sum(jnp.where(mine, found[f], 0.0), axis=0, keepdims=True) for f in range(TABLED)
     ]
+    if DIRECT:
+        plane_row = group_row + ((slot_row >> 7) << 6)
+        lane_row = slot_row & (CK - 1)
+        base = iota((CI, CK), 0)
+        pieces = [[] for _ in range(DIRECT)]
+        for c in range(0, C, CK):
+            plane = jnp.broadcast_to(plane_row[:, c : c + CK], (CI, CK))
+            lane = jnp.broadcast_to(lane_row[:, c : c + CK], (CI, CK))
+            total = [jnp.zeros((CI, CK), F32)] * DIRECT
+            for j in range(CJ):
+                here = base + CI * j == plane
+                for q in range(DIRECT):
+                    moved = jnp.take_along_axis(adj_ref[TABLED + q, j], lane, axis=1)
+                    total[q] = jnp.where(here, moved, total[q])
+            for q in range(DIRECT):
+                pieces[q].append(jnp.sum(total[q], axis=0, keepdims=True))
+        rows += [jnp.concatenate(p, 1) for p in pieces]
+    return rows
 
 
 def scatter_slots(values, base_i, base_j, base_t, x, y, z):
@@ -277,7 +300,9 @@
     count_ref,
     cell_ref,
     weight_ref,
-    out_ref,
+    z_hbm,
+    k_st,
+    k_state,
     table,
     where_ref,
     place,
@@ -300,11 +325,9 @@
     s_out,
     s_in,
     k_mat,
-    k_state,
     k_ends,
     k_pad,
     k_all,
-    k_st,
     xk,
     info_send,
     info_recv,
@@ -406,7 +429,7 @@
             jnp.concatenate([where_ref[a, pl.ds(o, 1), 0:HEAD] for o in owners], 1)
             for a in range(2)
         ]
-        rows = gather_slots(table, group_row, slot_row)
+        rows = gather_slots(adj_ref, table, group_row, slot_row)
         for n, o in enumerate(owners):
             live = iota((1, HEAD), 1) < count_ref[o]
             for f in range(FIELDS):
@@ -419,7 +442,7 @@
     lax.fori_loop(0, EARLY, owner_step, 0)
     incoming[block] = outgoing[block]
     for f, row in enumerate(
-        gather_slots(table, where_ref[0, pl.ds(hot, 1), HEAD:], where_ref[1, pl.ds(hot, 1), HEAD:])
+        gather_slots(adj_ref, table, where_ref[0, pl.ds(hot, 1), HEAD:], where_ref[1, pl.ds(hot, 1), HEAD:])
     ):
         rest[f : f + 1, :] = row
 
@@ -446,32 +469,35 @@
 
     lax.fori_loop(EARLY, BLOCKS // 2, late_step, 0)
 
-    over_peers(lambda d: info_copy(d).wait())
-    info = info_in[hot]
-    found = scatter_slots(
-        [rest[f : f + 1, :] for f in range(FIELDS)],
-        *donor_parts(info[0:1].astype(jnp.int32)),
-        info[1:2],
-        info[2:3],
-        info[3:4],
-    )
-    for p in range(BLOCKS):
-        acc_rest[p] = found[p * PART : (p + 1) * PART]
-    rs_in[block] = acc_rest[block]
-    over_peers(lambda d: rs_copy(d).start())
-
     acc[...] = jnp.zeros_like(acc)
 
     def source_step(t, carry):
-        sources = [lax.rem(block + BLOCKS - 2 * t - n, BLOCKS) for n in range(2)]
+        sources = [lax.rem(block + BLOCKS - TOGETHER * t - n, BLOCKS) for n in range(TOGETHER)]
 
         @pl.when(t > 0)
         def _():
-            slot_copy(2 * t).wait_recv()
-
-        slot_copy(2 * t + 1).wait_recv()
-
-        @pl.when(t == BLOCKS // 4)
+            slot_copy(TOGETHER * t).wait_recv()
+
+        for n in range(1, TOGETHER):
+            slot_copy(TOGETHER * t + n).wait_recv()
+
+        @pl.when(t == REST_AT)
+        def _():
+            over_peers(lambda d: info_copy(d).wait())
+            info = info_in[hot]
+            found = scatter_slots(
+                [rest[f : f + 1, :] for f in range(FIELDS)],
+                *donor_parts(info[0:1].astype(jnp.int32)),
+                info[1:2],
+                info[2:3],
+                info[3:4],
+            )
+            for p in range(BLOCKS):
+                acc_rest[p] = found[p * PART : (p + 1) * PART]
+            rs_in[block] = acc_rest[block]
+            over_peers(lambda d: rs_copy(d).start())
+
+        @pl.when(t == GRID_AT)
         def _():
             over_peers(lambda e: rs_copy(e).wait())
             total = rs_in[0]
@@ -497,7 +523,7 @@
         )
         return carry
 
-    lax.fori_loop(0, BLOCKS // 2, source_step, 0)
+    lax.fori_loop(0, BLOCKS // TOGETHER, source_step, 0)
     over_peers(lambda d: slot_copy(d).wait_send())
     over_peers(lambda d: ag_copy(d).wait())
 
@@ -579,6 +605,8 @@
         copy.start()
     for f in range(FIELDS):
         xk[f] = nt(stack3(xk[f], 1, False), k_mat[f])
+    store_z = pltpu.make_async_copy(xk, z_hbm, load_sem.at[2])
+    store_z.start()
     for copy in k_copies:
         copy.wait()
 
@@ -596,9 +624,24 @@
     for f in range(FIELDS):
         for a in range(4):
             k_st[f, a : a + 1, :] = kept[a // 2][a % 2][f : f + 1]
+    store_z.wait()
+
+
+def finish_kernel(z_ref, st_ref, state_ref, out_ref):
     for f in range(FIELDS):
-        done = xk[f] + mm_tn(k_st[f], k_state[f])
+        done = z_ref[f] + mm_tn(st_ref[f], state_ref[f])
         out_ref[f] = done[0 : CJ * CI].reshape(CJ, CI, CK)
+
+
+def finish(z, states, state_map):
+    vmem = pl.BlockSpec(memory_space=pltpu.VMEM)
+    return pl.pallas_call(
+        finish_kernel,
+        out_shape=jax.ShapeDtypeStruct((FIELDS, CJ, CI, CK), F32),
+        in_specs=[vmem] * 3,
+        out_specs=vmem,
+        name="finish",
+    )(z, states, state_map)
 
 
 def sweep(
@@ -618,11 +661,15 @@
     dma = pltpu.SemaphoreType.DMA
     return pl.pallas_call(
         main_kernel,
-        out_shape=jax.ShapeDtypeStruct((FIELDS, CJ, CI, CK), F32),
+        out_shape=[
+            jax.ShapeDtypeStruct((FIELDS, CK, CK), F32),
+            jax.ShapeDtypeStruct((FIELDS, 8, CK), F32),
+            jax.ShapeDtypeStruct((FIELDS, 8, CK), F32),
+        ],
         in_specs=[vmem] * 2 + [hbm, vmem, hbm, smem, smem] + [vmem] * 2,
-        out_specs=vmem,
+        out_specs=[hbm, vmem, vmem],
         scratch_shapes=[
-            pltpu.VMEM((FIELDS * 64, 512), BF),
+            pltpu.VMEM((TABLED * 64, 512), BF),
             pltpu.VMEM((2, BLOCKS, CAP), jnp.int32),
             pltpu.VMEM((3, BLOCKS, CAP), jnp.int32),
             pltpu.VMEM((BLOCKS, 32, 256), F32),
@@ -644,11 +691,9 @@
             pltpu.VMEM((LINES, 24, 256), F32),
             pltpu.VMEM((LINES, 24, 256), F32),
             pltpu.VMEM((FIELDS, CK, 3 * CK), BF),
-            pltpu.VMEM((FIELDS, 8, CK), F32),
             pltpu.VMEM((FIELDS, 8, 3 * CK), BF),
             pltpu.VMEM((FIELDS, 8, CK), F32),
             pltpu.VMEM((BLOCKS, 24, CK), F32),
-            pltpu.VMEM((FIELDS, 8, CK), F32),
             pltpu.VMEM((FIELDS, CK, CK), F32),
         ]
         + [dma((BLOCKS,))] * 8
@@ -657,7 +702,7 @@
         + [
             pltpu.VMEM((FIELDS, CJ, CI, CK), F32),
             pltpu.VMEM((2, FIELDS, CK, CK), F32),
-            dma((2,)),
+            dma((3,)),
         ],
         compiler_params=pltpu.CompilerParams(
             vmem_limit_bytes=56 * 2**20, collective_id=0, has_side_effects=True
@@ -687,7 +732,7 @@
     donor_cell,
     donor_weight,
 ):
-    update = sweep(
+    update = finish(*sweep(
         adjoint.transpose(0, 2, 1, 3),
         receptor_cell[0, 0],
         residual.transpose(0, 2, 1, 3),
@@ -697,7 +742,7 @@
         send_count[0, 0],
         donor_cell[0, 0],
         donor_weight[0, 0],
-    )
+    ))
     return update.transpose(0, 2, 1, 3)
 
 

time: 54.5 us -> 53.2 us (0.976)
  local copies, waits for them, and re-layouts: 1.75 us -> 0 us
    unnamed x1 -> x0, local copies, waits for them, and re-layouts: 1.75 us -> none
    pallas_call x1 -> x2, Pallas kernels: 52.5 us -> 53 us  [the longest x1 50.7 us: sweep(): pl.pallas_call(main_kernel, out_shape=[jax.ShapeDtypeStruct((FIELDS, CK,...]
where the time goes in v4:
time: 53.2 us; the launch traced here: 53 us
  Pallas kernels  53 us (100%)
    pallas_call x1, Pallas kernels, sweep(): pl.pallas_call(main_kernel, out_shape=[jax.ShapeDtypeStruct((FIELDS, CK,...  50.7 us
    pallas_call x1, Pallas kernels, finish(): pl.pallas_call(finish_kernel, out_shape=jax.ShapeDtypeStruct((FIELDS, CJ,...  2.3 us

profile of v4, /device:TPU:0, one launch (start us, length us, event | category | flops | bytes accessed | tf_op | source)
XLA Modules:
  0.0 53.0 jit_solution(15036192037119641575)
XLA Ops:
  0.0 50.7 %sweep.1 = (f32[6,128,128]{2,1,0:T(8,128)}, f32[6,8,128]{2,1,0:T(8,128)}, f32[6,8,128]{2,1,0:T(8,128)}) custom-call(f32[6,15,8,128]{3,2,1,0:T(8,128)} %bitcast.14, s32[16,2048]{1,0:T(8,128)} %bitcast.16, f32[6,15,8,128]{3,2,1,0:T(8,128)} %bitcast.15, f32[2,6,8,8]{3,2,1,0:T(8,128)} %bitcast.18, f32[2,6,128,128]{3,2,1,0:T(8,128)} %bitcast.12, ...), custom_call_target="tpu_custom_call" | custom-call | tf_op jit(solution)/shard_map/sweep/pallas_call | solution.py:662
  50.7 2.3 %finish.1 = f32[6,15,8,128]{3,2,1,0:T(8,128)} custom-call(f32[6,128,128]{2,1,0:T(8,128)} %get-tuple-element.8.z_ref, f32[6,8,128]{2,1,0:T(8,128)} %get-tuple-element.9.st_ref, f32[6,8,128]{2,1,0:T(8,128)} %get-tuple-element.10.state_ref), custom_call_target="tpu_custom_call" | custom-call | tf_op jit(solution)/shard_map/finish/pallas_call | solution.py:638

commit v5 on v4

--- a/solution.py
+++ b/solution.py
@@ -212,6 +212,16 @@
 
 def nt(a, b):
     return lax.dot_general(a, b, (((1,), (1,)), ((), ())), preferred_element_type=F32)
+
+
+def mm_fast(a, b):
+    a_high, a_low = split(a)
+    b_high, b_low = split(b)
+
+    def one(p, q):
+        return jnp.dot(p, q, preferred_element_type=F32)
+
+    return one(a_high, b_high) + one(a_high, b_low) + one(a_low, b_high)
 
 
 def mm3_nt(a, b):
@@ -540,17 +550,17 @@
         x[:, j * CK : (j + 1) * CK] = total
     x[:, CJ * CK :] = jnp.zeros((n, CK), F32)
 
-    ends = mm(i_ends[...], x[...])
+    ends = mm_fast(i_ends[...], x[...])
     for c in range(LINES):
         i_out[c] = ends[:, c * 256 : (c + 1) * 256]
     i_in[line] = i_out[line]
     end_copies = [
         to_line(d, i_out.at[(line + d) % LINES], i_in.at[line], end_send, end_recv)
-        for d in range(1, LINES)
+        for d in (4, 5, 3, 6, 2, 7, 1)
     ]
     for copy in end_copies:
         copy.start()
-    x[...] = mm(i_mat[...], x[...])
+    x[...] = mm_fast(i_mat[...], x[...])
     k_refs = (kfac_ref, coup_ref, k_mat, k_state, k_ends, k_pad)
     prepare_k(range(0, 3), *k_refs)
     for copy in map_copies:
@@ -572,7 +582,7 @@
     s_in[line] = s_out[line]
     st_copies = [
         to_line(d, s_out.at[(line + d) % LINES], s_in.at[line], st_send, st_recv)
-        for d in range(1, LINES)
+        for d in (4, 5, 3, 6, 2, 7, 1)
     ]
     for copy in st_copies:
         copy.start()
@@ -580,7 +590,7 @@
     for copy in st_copies:
         copy.wait()
     for c in range(LINES):
-        part = x[:, c * 256 : (c + 1) * 256] + mm(i_state[...], s_in[c])
+        part = x[:, c * 256 : (c + 1) * 256] + mm_fast(i_state[...], s_in[c])
         for jj in range(2):
             j = 2 * c + jj
             for f in range(FIELDS):
@@ -599,7 +609,7 @@
             device_id={"block": (block + d) % BLOCKS},
             device_id_type=MESH,
         )
-        for d in range(1, BLOCKS)
+        for d in (10, 9, 11, 6, 14, 5, 7, 13, 2, 8, 15, 3, 1, 4, 12)
     ]
     for copy in k_copies:
         copy.start()

time: 53.2 us -> 52.9 us (level)
  no operation moved by 1% of the time
where the time goes in v5:
time: 52.9 us; the launch traced here: 52.7 us
  Pallas kernels  52.7 us (100%)
    pallas_call x1, Pallas kernels, sweep(): pl.pallas_call(main_kernel, out_shape=[jax.ShapeDtypeStruct((FIELDS, CK,...  50.4 us
    pallas_call x1, Pallas kernels, finish(): pl.pallas_call(finish_kernel, out_shape=jax.ShapeDtypeStruct((FIELDS, CJ,...  2.3 us

profile of v5, /device:TPU:0, one launch (start us, length us, event | category | flops | bytes accessed | tf_op | source)
XLA Modules:
  0.0 52.7 jit_solution(6699005208392519033)
XLA Ops:
  0.0 50.4 %sweep.1 = (f32[6,128,128]{2,1,0:T(8,128)}, f32[6,8,128]{2,1,0:T(8,128)}, f32[6,8,128]{2,1,0:T(8,128)}) custom-call(f32[6,15,8,128]{3,2,1,0:T(8,128)} %bitcast.14, s32[16,2048]{1,0:T(8,128)} %bitcast.16, f32[6,15,8,128]{3,2,1,0:T(8,128)} %bitcast.15, f32[2,6,8,8]{3,2,1,0:T(8,128)} %bitcast.18, f32[2,6,128,128]{3,2,1,0:T(8,128)} %bitcast.12, ...), custom_call_target="tpu_custom_call" | custom-call | tf_op jit(solution)/shard_map/sweep/pallas_call | solution.py:672
  50.4 2.3 %finish.1 = f32[6,15,8,128]{3,2,1,0:T(8,128)} custom-call(f32[6,128,128]{2,1,0:T(8,128)} %get-tuple-element.8.z_ref, f32[6,8,128]{2,1,0:T(8,128)} %get-tuple-element.9.st_ref, f32[6,8,128]{2,1,0:T(8,128)} %get-tuple-element.10.state_ref), custom_call_target="tpu_custom_call" | custom-call | tf_op jit(solution)/shard_map/finish/pallas_call | solution.py:648
